TPU v7x, 32 devices: a whole 2x2x4 slice. The times are simulated.
32 devices in a mesh: groups: 2 (over y), lon: 16 (over z, x, core).
Axes of the slice: x: 2, y: 2, z: 4, core: 2. Of those that a mesh axis runs over, the one named last changes fastest.
Arguments:
- celerity: float32 [512, 2048], P('lon'), may hold values from 0.1 to 0.45
- station_tile: int32 [65536, 1], P(('groups', 'lon')), parts along dimension 0, may hold values from 0 to 15; in each aligned block of 2048 rows (0 to 2047, 2048 to 4095, ...) at most 256 rows name the same one
- station_block: int32 [65536], P(('groups', 'lon')), parts along dimension 0, may hold values from 0 to 511
- footprint: bfloat16 [65536, 128], P(('groups', 'lon')), parts along dimension 0, may hold values from 0 to 1
- misfit: bfloat16 [8, 65536], P(None, ('groups', 'lon')), parts along dimension 1, may hold values from -1.1953125 to 1.1953125
- segment_block: int32 [1024], P('lon'), may hold values from 0 to 511
- segment_fault: int32 [1024], P('lon'), may hold values from 0 to 63
- green_uplift: bfloat16 [1024, 256], P('lon'), may hold values from -0.5 to 0.5
Outputs:
- adjoint: float32 [1024, 2048], P(('groups', 'lon')), parts along dimension 0
- gradient: float32 [128, 64], P(('groups', 'lon')), parts along dimension 0
There are 2 independent parts, one for each index of `groups`. A program takes and returns all parts, laid end to end along the dimension named above; an argument that names none is the same for every part. Nothing has to cross between parts.
Inputs may be any that keep to these rules, and one draw needn't show every extreme that they name: `station_tile`: in each aligned block of the 2048 observations of one device, no tile is named more than 256 times, a bound that some block reaches.
All inputs are finite; a program needn't handle non-finite values.
Results may differ from a plain program's by a relative error of at most 0.0003.
Values may be sent and summed in bfloat16 or wider, within the bound.
A program may use at most 64 MiB of HBM per device.

v0:
```python
import functools

import jax
import jax.numpy as jnp
from jax import lax
from jax.experimental import pallas as pl
from jax.experimental.pallas import tpu as pltpu
from jax.sharding import PartitionSpec as P

SUB_DEV = 4
NWIN = 32
LANES = 128
RIM = 8
META = 16
HIGH = lax.Precision.HIGHEST


def iota(shape, dim):
    return lax.broadcasted_iota(jnp.int32, shape, dim)


def order(turn, tiles):
    half = tiles // 2
    swing = (turn + 1) // 2
    shift = half + jnp.where(lax.rem(turn, 2) == 1, -swing, swing)
    return jnp.where(turn == tiles - 1, 0, shift)


def kernel(
    tiles,
    cap,
    cel_ref,
    tile_ref,
    block_ref,
    foot_ref,
    mis_ref,
    segb_ref,
    segf_ref,
    green_ref,
    out_ref,
    grad_ref,
    ext,
    placed,
    sent,
    got,
    field,
    rim_out,
    rim_in,
    cel_in,
    past,
    picks,
    part_out,
    part_in,
    send_sem,
    recv_sem,
    rim_send,
    rim_recv,
    cel_send,
    cel_recv,
    part_send,
    part_recv,
):
    me = lax.axis_index("lon")
    rows, lat = cel_ref.shape
    stations = foot_ref.shape[0]
    steps = mis_ref.shape[0]
    segments = green_ref.shape[0]
    chunks = lat // LANES
    wide = rows + 2 * RIM
    pages = -(-cap // LANES)
    page = min(cap, LANES)
    own = slice(RIM, RIM + rows)
    barrier = pltpu.get_barrier_semaphore()

    def partner(shift):
        return lax.rem(me + shift, tiles)

    def greet(shift, carry):
        pl.semaphore_signal(
            barrier,
            inc=1,
            device_id={"lon": partner(shift)},
            device_id_type=pl.DeviceIdType.MESH,
        )
        return carry

    lax.fori_loop(1, tiles, greet, 0)

    span = min(256, stations)
    ramp = (iota((span, span), 0) < iota((span, span), 1)).astype(jnp.bfloat16)
    carry = jnp.zeros((tiles, 1), jnp.float32)
    for start in range(0, stations, span):
        target = tile_ref[:, start : start + span]
        hot = iota((tiles, span), 0) == target
        ones = jnp.where(hot, 1.0, 0.0)
        before = carry + jnp.dot(
            ones.astype(jnp.bfloat16), ramp, preferred_element_type=jnp.float32
        )
        ranked = jnp.sum(jnp.where(hot, before, 0.0), axis=0, keepdims=True)
        placed[:, start : start + span] = target * cap + ranked.astype(jnp.int32)
        carry = carry + jnp.sum(ones, axis=1, keepdims=True)

    blocks = block_ref[...]
    row = lax.div(blocks, chunks).astype(jnp.float32)
    chunk = lax.rem(blocks, chunks).astype(jnp.float32)
    place = iota((8, stations), 0)
    digits = jnp.where(place == 0, row, jnp.where(place == 1, chunk, 0.0))
    meta = jnp.concatenate(
        [
            mis_ref[...].astype(jnp.float32),
            digits,
            jnp.zeros((LANES - steps - 8, stations), jnp.float32),
        ],
        axis=0,
    )
    ext[:, :LANES] = foot_ref[...]
    ext[:, LANES:] = meta.T.astype(jnp.bfloat16)
    field[...] = jnp.zeros_like(field)

    pl.semaphore_wait(barrier, tiles - 1)

    def side_copy(side, source, landing, send, recv):
        return pltpu.make_async_remote_copy(
            src_ref=source,
            dst_ref=landing,
            send_sem=send.at[side],
            recv_sem=recv.at[side],
            device_id={"lon": me - 1 if side == 0 else me + 1},
            device_id_type=pl.DeviceIdType.MESH,
        )

    exists = (me > 0, me < tiles - 1)

    def cel_copy(side):
        rim = slice(0, RIM) if side == 0 else slice(rows - RIM, rows)
        return side_copy(side, cel_ref.at[rim], cel_in.at[side], cel_send, cel_recv)

    def rim_copy(side):
        return side_copy(side, rim_out.at[side], rim_in.at[side], rim_send, rim_recv)

    for side in range(2):

        @pl.when(exists[side])
        def _():
            cel_copy(side).start()

    def obs_copy(turn):
        return pltpu.make_async_remote_copy(
            src_ref=sent.at[turn],
            dst_ref=got.at[turn],
            send_sem=send_sem.at[turn],
            recv_sem=recv_sem.at[turn],
            device_id={"lon": partner(order(turn, tiles))},
            device_id_type=pl.DeviceIdType.MESH,
        )

    def pack(turn, box):
        base = partner(order(turn, tiles)) * cap
        slot_hot = placed[...] == base + iota((cap, stations), 0)
        matrix = jnp.where(slot_hot, 1.0, 0.0).astype(jnp.bfloat16)
        packed = jnp.dot(matrix, ext[...], preferred_element_type=jnp.float32)
        box[turn, :cap, :] = packed[:, :LANES].astype(jnp.bfloat16)
        turned = packed[:, LANES:].T
        for n in range(pages):
            box[turn, cap + n * META : cap + (n + 1) * META, :page] = turned[
                :META, n * page : (n + 1) * page
            ].astype(jnp.bfloat16)

    def pack_and_send(turn, carry):
        pack(turn, sent)
        obs_copy(turn).start()
        return carry

    lax.fori_loop(0, tiles - 1, pack_and_send, 0)
    pack(tiles - 1, got)

    def spread(turn):
        sheets = [
            got[turn, cap + n * META : cap + (n + 1) * META, :][:, :page].astype(jnp.float32)
            for n in range(pages)
        ]
        meta = sheets[0] if pages == 1 else jnp.concatenate(sheets, axis=1)
        key = meta[steps + 1 : steps + 2] * rows + meta[steps : steps + 1]
        hot = key.astype(jnp.int32) == iota((rows * chunks, cap), 0)
        prints = got[turn, :cap, :]
        for moment in range(steps):
            weighted = jnp.where(hot, meta[moment : moment + 1], 0.0).astype(jnp.bfloat16)
            summed = jnp.dot(weighted, prints, preferred_element_type=jnp.float32)
            for c in range(chunks):
                cells = (moment, own, slice(c * LANES, (c + 1) * LANES))
                field[cells] = field[cells] + summed[c * rows : (c + 1) * rows]

    spread(tiles - 1)

    def receive(turn, carry):
        obs_copy(turn).wait_recv()
        spread(turn)
        return carry

    lax.fori_loop(0, tiles - 1, receive, 0)

    last = steps - 1
    level = iota((RIM, lat), 0)
    for n in range(steps // 2):
        t = last - n
        head, tail = field[t, own][:RIM], field[last - t, own][:RIM]
        rim_out[0, n] = jnp.where(level < t, head, pltpu.roll(tail, t, 0))
        head, tail = field[t, own][rows - RIM :], field[last - t, own][rows - RIM :]
        rim_out[1, n] = jnp.where(level >= RIM - t, head, pltpu.roll(tail, RIM - t, 0))
    for side in range(2):

        @pl.when(exists[side])
        def _():
            rim_copy(side).start()

    for side in range(2):

        @pl.when(exists[1 - side])
        def _():
            cel_copy(side).wait_recv()

        @pl.when(jnp.logical_not(exists[1 - side]))
        def _():
            cel_in[side] = jnp.zeros((RIM, lat), jnp.float32)

    kappa = jnp.concatenate([cel_in[1], cel_ref[...], cel_in[0]], axis=0)
    column = iota((wide, lat), 1)
    line = iota((wide, lat), 0) + (me * rows - RIM)
    inside = jnp.logical_and(line >= 0, line < tiles * rows)
    north = 0.5 * (kappa + pltpu.roll(kappa, 1, 0))
    south = 0.5 * (kappa + pltpu.roll(kappa, wide - 1, 0))
    west_edge, east_edge = column == 0, column == lat - 1
    west = 0.5 * (kappa + jnp.where(west_edge, 0.0, pltpu.roll(kappa, 1, 1)))
    east = 0.5 * (kappa + jnp.where(east_edge, 0.0, pltpu.roll(kappa, lat - 1, 1)))
    centre = 2.0 - (north + south + west + east)
    west = jnp.where(west_edge, 0.0, west)
    east = jnp.where(east_edge, 0.0, east)

    for side in range(2):

        @pl.when(exists[1 - side])
        def _():
            rim_copy(side).wait_recv()
            for n in range(steps // 2):
                t = last - n
                tile = rim_in[side, n]
                if side == 0:
                    rim = slice(RIM + rows, wide)
                    field[t, rim] = jnp.where(level < t, tile, 0.0)
                    field[last - t, rim] = jnp.where(
                        level < last - t, pltpu.roll(tile, RIM - t, 0), 0.0
                    )
                else:
                    rim = slice(0, RIM)
                    field[t, rim] = jnp.where(level >= RIM - t, tile, 0.0)
                    field[last - t, rim] = jnp.where(level > t, pltpu.roll(tile, t, 0), 0.0)

    def keep(t, surface):
        for c in range(chunks):
            past[t, c] = surface[own, c * LANES : (c + 1) * LANES]

    keep(last, field[last])

    def advance(step, carry):
        t = last - step
        current = field[t + 1]
        moved = (
            centre * current
            + north * pltpu.roll(current, 1, 0)
            + south * pltpu.roll(current, wide - 1, 0)
            + west * pltpu.roll(current, 1, 1)
            + east * pltpu.roll(current, lat - 1, 1)
            + field[t]
        )
        previous = field[jnp.minimum(t + 2, last)]
        moved = moved - jnp.where(step > 1, previous, 0.0)
        fresh = jnp.where(inside, moved, 0.0)
        field[t] = fresh
        keep(t, fresh)
        return carry

    lax.fori_loop(1, steps, advance, 0)
    out_ref[...] = field[0, own]

    def pick(segment, carry):
        block = segb_ref[segment]
        line, chunk = lax.div(block, chunks), lax.rem(block, chunks)
        for t in range(steps):
            picks[t, pl.ds(segment, 1)] = past[t, chunk, pl.ds(line, 1)]
        return carry

    lax.fori_loop(0, segments, pick, 0)

    lines = tiles * 8
    number = iota((lines, segments), 0)
    fault = jnp.where(
        lax.rem(number, 8) < SUB_DEV, lax.div(number, 8) * SUB_DEV + lax.rem(number, 8), -1
    )
    owner_hot = jnp.where(segf_ref[...] == fault, 1.0, 0.0)
    green = green_ref[...].astype(jnp.float32)
    moment = lax.div(iota((steps * LANES, LANES), 0), LANES).astype(jnp.float32)
    window = iota((steps * LANES, LANES), 1)
    tent_at = lax.rem(window, NWIN).astype(jnp.float32) * (steps - 1) / (NWIN - 1)
    tent = jnp.maximum(0.0, 1.0 - jnp.abs(moment - tent_at))
    total = None
    for rake in range(2):
        weights = green[:, rake * LANES : (rake + 1) * LANES]
        products = jnp.concatenate([picks[t] * weights for t in range(steps)], axis=1)
        by_fault = jnp.dot(owner_hot, products, precision=HIGH, preferred_element_type=jnp.float32)
        basis = jnp.where(lax.div(window, NWIN) == rake, tent, 0.0)
        term = jnp.dot(by_fault, basis, precision=HIGH, preferred_element_type=jnp.float32)
        total = term if total is None else total + term
    part_out[...] = total.reshape(tiles, 8, LANES)

    def part_copy(turn):
        there = partner(order(turn, tiles))
        return pltpu.make_async_remote_copy(
            src_ref=part_out.at[there],
            dst_ref=part_in.at[turn],
            send_sem=part_send.at[turn],
            recv_sem=part_recv.at[turn],
            device_id={"lon": there},
            device_id_type=pl.DeviceIdType.MESH,
        )

    def part_start(turn, carry):
        part_copy(turn).start()
        return carry

    lax.fori_loop(0, tiles - 1, part_start, 0)
    part_in[tiles - 1] = part_out[me]

    def sent_wait(turn, carry):
        obs_copy(turn).wait_send()
        return carry

    lax.fori_loop(0, tiles - 1, sent_wait, 0)
    for side in range(2):

        @pl.when(exists[side])
        def _():
            cel_copy(side).wait_send()
            rim_copy(side).wait_send()

    def part_wait(turn, carry):
        part_copy(turn).wait()
        return carry

    lax.fori_loop(0, tiles - 1, part_wait, 0)
    grad_ref[...] = jnp.sum(part_in[...], axis=0)[:SUB_DEV, : 2 * NWIN]


def local(
    celerity,
    station_tile,
    station_block,
    footprint,
    misfit,
    segment_block,
    segment_fault,
    green_uplift,
):
    tiles = lax.axis_size("lon")
    rows, lat = celerity.shape
    stations = footprint.shape[0]
    steps = misfit.shape[0]
    segments = green_uplift.shape[0]
    cap = 2 * stations // tiles
    depth = cap + META * -(-cap // LANES)
    dma = pltpu.SemaphoreType.DMA
    vmem = pl.BlockSpec(memory_space=pltpu.VMEM)
    return pl.pallas_call(
        functools.partial(kernel, tiles, cap),
        out_shape=(
            jax.ShapeDtypeStruct((rows, lat), jnp.float32),
            jax.ShapeDtypeStruct((SUB_DEV, 2 * NWIN), jnp.float32),
        ),
        in_specs=[vmem] * 5 + [pl.BlockSpec(memory_space=pltpu.SMEM)] + [vmem] * 2,
        out_specs=(vmem, vmem),
        scratch_shapes=[
            pltpu.VMEM((stations, 2 * LANES), jnp.bfloat16),
            pltpu.VMEM((1, stations), jnp.int32),
            pltpu.VMEM((tiles, depth, LANES), jnp.bfloat16),
            pltpu.VMEM((tiles, depth, LANES), jnp.bfloat16),
            pltpu.VMEM((steps, rows + 2 * RIM, lat), jnp.float32),
            pltpu.VMEM((2, steps // 2, RIM, lat), jnp.float32),
            pltpu.VMEM((2, steps // 2, RIM, lat), jnp.float32),
            pltpu.VMEM((2, RIM, lat), jnp.float32),
            pltpu.VMEM((steps, lat // LANES, rows, LANES), jnp.float32),
            pltpu.VMEM((steps, segments, LANES), jnp.float32),
            pltpu.VMEM((tiles, 8, LANES), jnp.float32),
            pltpu.VMEM((tiles, 8, LANES), jnp.float32),
            dma((tiles,)),
            dma((tiles,)),
            dma((2,)),
            dma((2,)),
            dma((2,)),
            dma((2,)),
            dma((tiles,)),
            dma((tiles,)),
        ],
        compiler_params=pltpu.CompilerParams(
            collective_id=0, has_side_effects=True, vmem_limit_bytes=44 * 1024 * 1024
        ),
    )(
        celerity,
        station_tile.reshape(1, stations),
        station_block.reshape(1, stations),
        footprint,
        misfit,
        segment_block,
        segment_fault.reshape(1, segments),
        green_uplift,
    )


def solution(mesh):
    placed = (
        P("lon", None),
        P(("groups", "lon"), None),
        P(("groups", "lon")),
        P(("groups", "lon"), None),
        P(None, ("groups", "lon")),
        P("lon"),
        P("lon"),
        P("lon", None),
    )
    return jax.shard_map(
        local,
        mesh=mesh,
        in_specs=placed,
        out_specs=(P(("groups", "lon"), None), P(("groups", "lon"), None)),
        check_vma=False,
    )
```

profile of v0, /device:TPU:0, one launch (start us, length us, event | category | flops | bytes accessed | tf_op | source)
XLA Modules:
  0.0 63.3 jit_solution(18021860074062523009)
XLA Ops:
  0.6 0.0 copy-start.6
  0.6 0.0 copy-start.7
  0.7 0.6 %copy-done.6 = s32[64]{0:T(128)S(1)} copy-done((s32[64]{0:T(128)S(1)}, s32[64]{0:T(128)}, u32[]{:S(2)}) %copy-start.6) | copy-done | bytes 280
  1.3 0.0 copy-done.7
  1.3 0.0 copy-start
  1.3 1.0 %copy-done = bf16[2048,128]{1,0:T(8,128)(2,1)S(1)} copy-done((bf16[2048,128]{1,0:T(8,128)(2,1)S(1)}, bf16[2048,128]{1,0:T(8,128)(2,1)}, u32[]{:S(2)}) %copy-start) | copy-done | bytes 524312
  2.3 0.0 copy-start.1
  2.3 0.9 %copy-done.1 = f32[32,2048]{1,0:T(8,128)S(1)} copy-done((f32[32,2048]{1,0:T(8,128)S(1)}, f32[32,2048]{1,0:T(8,128)}, u32[]{:S(2)}) %copy-start.1) | copy-done | bytes 262168
  3.3 0.0 copy-start.2
  3.3 0.8 %copy-done.2 = bf16[8,2048]{1,0:T(8,128)(2,1)S(1)} copy-done((bf16[8,2048]{1,0:T(8,128)(2,1)S(1)}, bf16[8,2048]{1,0:T(8,128)(2,1)}, u32[]{:S(2)}) %copy-start.2) | copy-done | bytes 32792
  4.1 0.0 copy-start.3
  4.1 0.8 %copy-done.3 = bf16[64,256]{1,0:T(8,128)(2,1)S(1)} copy-done((bf16[64,256]{1,0:T(8,128)(2,1)S(1)}, bf16[64,256]{1,0:T(8,128)(2,1)}, u32[]{:S(2)}) %copy-start.3) | copy-done | bytes 32792
  4.8 0.0 copy-start.4
  4.8 0.7 %copy-done.4 = s32[2048,1]{0,1:T(1,128)S(1)} copy-done((s32[2048,1]{0,1:T(1,128)S(1)}, s32[2048,1]{0,1:T(1,128)}, u32[]{:S(2)}) %copy-start.4) | copy-done | bytes 8216
  5.5 0.0 copy-start.5
  5.5 0.7 %copy-done.5 = s32[2048]{0:T(1024)S(1)} copy-done((s32[2048]{0:T(1024)S(1)}, s32[2048]{0:T(1024)}, u32[]{:S(2)}) %copy-start.5) | copy-done | bytes 8216
  6.2 55.8 %shard_map.95 = (f32[32,2048]{1,0:T(8,128)S(1)}, f32[4,64]{1,0:T(4,128)S(1)}) custom-call(f32[32,2048]{1,0:T(8,128)S(1)} %copy-done.1, s32[1,2048]{1,0:T(1,128)S(1)} %bitcast.3, s32[1,2048]{1,0:T(1,128)S(1)} %bitcast.4, bf16[2048,128]{1,0:T(8,128)(2,1)S(1)} %copy-done, bf16[8,2048]{1,0:T(8,128)(2,1)S(1)} %copy-done.2, s32[64]{0:T(128)S(1)} %copy-done.6, ...), custom_call_target="tpu_custom_call" | custom-call | tf_op jit(solution)/shard_map/pallas_call | solution.py:372
  62.0 0.7 %copy.12 = f32[32,2048]{1,0:T(8,128)} copy(f32[32,2048]{1,0:T(8,128)S(1)} %get-tuple-element.4) | data formatting | bytes 524288
  62.7 0.6 copy.13
Async XLA Ops:
  0.6 0.7 %copy-start.6 = (s32[64]{0:T(128)S(1)}, s32[64]{0:T(128)}, u32[]{:S(2)}) copy-start(s32[64]{0:T(128)} %segb_ref.1) | copy-start | bytes 772
  0.6 0.7 %copy-start.7 = (s32[64]{0:T(128)S(1)}, s32[64]{0:T(128)}, u32[]{:S(2)}) copy-start(s32[64]{0:T(128)} %param.14) | copy-start | bytes 772
  1.3 1.0 %copy-start = (bf16[2048,128]{1,0:T(8,128)(2,1)S(1)}, bf16[2048,128]{1,0:T(8,128)(2,1)}, u32[]{:S(2)}) copy-start(bf16[2048,128]{1,0:T(8,128)(2,1)} %foot_ref.1) | copy-start | bytes 1572868
  2.3 0.9 %copy-start.1 = (f32[32,2048]{1,0:T(8,128)S(1)}, f32[32,2048]{1,0:T(8,128)}, u32[]{:S(2)}) copy-start(f32[32,2048]{1,0:T(8,128)} %cel_ref.1) | copy-start | bytes 786436
  3.3 0.8 %copy-start.2 = (bf16[8,2048]{1,0:T(8,128)(2,1)S(1)}, bf16[8,2048]{1,0:T(8,128)(2,1)}, u32[]{:S(2)}) copy-start(bf16[8,2048]{1,0:T(8,128)(2,1)} %mis_ref.1) | copy-start | bytes 98308
  4.1 0.8 %copy-start.3 = (bf16[64,256]{1,0:T(8,128)(2,1)S(1)}, bf16[64,256]{1,0:T(8,128)(2,1)}, u32[]{:S(2)}) copy-start(bf16[64,256]{1,0:T(8,128)(2,1)} %green_ref.1) | copy-start | bytes 98308
  4.8 0.7 %copy-start.4 = (s32[2048,1]{0,1:T(1,128)S(1)}, s32[2048,1]{0,1:T(1,128)}, u32[]{:S(2)}) copy-start(s32[2048,1]{0,1:T(1,128)} %param.9) | copy-start | bytes 24580
  5.5 0.7 %copy-start.5 = (s32[2048]{0:T(1024)S(1)}, s32[2048]{0:T(1024)}, u32[]{:S(2)}) copy-start(s32[2048]{0:T(1024)} %param.10) | copy-start | bytes 24580
where the time goes:
time: 63.7 us; the launch traced here: 63.3 us
  Pallas kernels  55.8 us (88%)
  local copies, waits for them, and re-layouts  6.84 us (11%)
  between operations  0.66 us (1%)
    pallas_call x1, Pallas kernels, local(): pl.pallas_call(functools.partial(kernel, tiles, cap), out_shape=(jax.Shap...  55.8 us
    unnamed x18, local copies, waits for them, and re-layouts  6.84 us

commit v1 on v0

v1 whole, which is shorter than its diff:
```python
import functools

import jax
import jax.numpy as jnp
from jax import lax
from jax.experimental import pallas as pl
from jax.experimental.pallas import tpu as pltpu
from jax.sharding import PartitionSpec as P

SUB_DEV = 4
NWIN = 32
LANES = 128
RIM = 8
META = 16
HIGH = lax.Precision.HIGHEST


def iota(shape, dim):
    return lax.broadcasted_iota(jnp.int32, shape, dim)


def order(turn, tiles):
    half = tiles // 2
    return jnp.where(lax.rem(turn, 2) == 0, half + lax.div(turn, 2), lax.div(turn + 1, 2))


def kernel(
    tiles,
    cap,
    cel_hbm,
    tile_hbm,
    block_hbm,
    foot_hbm,
    mis_hbm,
    segb_hbm,
    segf_hbm,
    green_hbm,
    out_ref,
    grad_ref,
    tile_ref,
    block_ref,
    mis_ref,
    segb_ref,
    segf_ref,
    green_ref,
    kappa_ref,
    coef,
    basis,
    load_sem,
    ext,
    placed,
    sent,
    got,
    field,
    rim_out,
    rim_in,
    past,
    picks,
    part_out,
    part_in,
    send_sem,
    recv_sem,
    rim_send,
    rim_recv,
    cel_send,
    cel_recv,
    part_send,
    part_recv,
):
    me = lax.axis_index("lon")
    rows, lat = cel_hbm.shape
    stations = foot_hbm.shape[0]
    steps = mis_hbm.shape[0]
    segments = green_hbm.shape[0]
    chunks = lat // LANES
    wide = rows + 2 * RIM
    pages = -(-cap // LANES)
    page = min(cap, LANES)
    own = slice(RIM, RIM + rows)
    barrier = pltpu.get_barrier_semaphore()

    loads = [
        pltpu.make_async_copy(source, landing, load_sem.at[n])
        for n, (source, landing) in enumerate(
            (
                (tile_hbm, tile_ref),
                (block_hbm, block_ref),
                (mis_hbm, mis_ref),
                (foot_hbm, ext.at[:, pl.ds(0, LANES)]),
                (cel_hbm, kappa_ref.at[pl.ds(RIM, rows)]),
                (segb_hbm, segb_ref),
                (segf_hbm, segf_ref),
                (green_hbm, green_ref),
            )
        )
    ]
    for load in loads:
        load.start()

    def partner(code):
        there, unit = 0, 1
        while unit < tiles:
            there += lax.rem(lax.div(me, unit) + lax.div(code, unit), 2) * unit
            unit *= 2
        return there

    def greet(shift, carry):
        pl.semaphore_signal(
            barrier,
            inc=1,
            device_id={"lon": partner(shift)},
            device_id_type=pl.DeviceIdType.MESH,
        )
        return carry

    lax.fori_loop(1, tiles, greet, 0)
    for load in loads[:3]:
        load.wait()

    span = min(256, stations)
    ramp = (iota((span, span), 0) < iota((span, span), 1)).astype(jnp.bfloat16)
    carry = jnp.zeros((tiles, 1), jnp.float32)
    for start in range(0, stations, span):
        target = tile_ref[:, start : start + span]
        hot = iota((tiles, span), 0) == target
        ones = jnp.where(hot, 1.0, 0.0)
        before = carry + jnp.dot(
            ones.astype(jnp.bfloat16), ramp, preferred_element_type=jnp.float32
        )
        ranked = jnp.sum(jnp.where(hot, before, 0.0), axis=0, keepdims=True)
        placed[:, start : start + span] = target * cap + ranked.astype(jnp.int32)
        carry = carry + jnp.sum(ones, axis=1, keepdims=True)

    blocks = block_ref[...]
    row = lax.div(blocks, chunks).astype(jnp.float32)
    chunk = lax.rem(blocks, chunks).astype(jnp.float32)
    place = iota((8, stations), 0)
    digits = jnp.where(place == 0, row, jnp.where(place == 1, chunk, 0.0))
    meta = jnp.concatenate(
        [
            mis_ref[...].astype(jnp.float32),
            digits,
            jnp.zeros((LANES - steps - 8, stations), jnp.float32),
        ],
        axis=0,
    )
    ext[:, LANES:] = meta.T.astype(jnp.bfloat16)
    loads[3].wait()

    pl.semaphore_wait(barrier, tiles - 1)

    def side_copy(side, source, landing, send, recv):
        return pltpu.make_async_remote_copy(
            src_ref=source,
            dst_ref=landing,
            send_sem=send.at[side],
            recv_sem=recv.at[side],
            device_id={"lon": me - 1 if side == 0 else me + 1},
            device_id_type=pl.DeviceIdType.MESH,
        )

    exists = (me > 0, me < tiles - 1)

    def cel_copy(side):
        source = cel_hbm.at[pl.ds(0 if side == 0 else rows - RIM, RIM)]
        landing = kappa_ref.at[pl.ds(RIM + rows if side == 0 else 0, RIM)]
        return side_copy(side, source, landing, cel_send.at[0], cel_recv.at[0])

    def rim_copy(side, n):
        return side_copy(
            side, rim_out.at[side, n], rim_in.at[side, n], rim_send.at[n], rim_recv.at[n]
        )

    for side in range(2):

        @pl.when(exists[side])
        def _():
            cel_copy(side).start()

    def obs_copy(code):
        return pltpu.make_async_remote_copy(
            src_ref=sent.at[code],
            dst_ref=got.at[code],
            send_sem=send_sem.at[code],
            recv_sem=recv_sem.at[code],
            device_id={"lon": partner(code)},
            device_id_type=pl.DeviceIdType.MESH,
        )

    def pack(code, there, box):
        slot_hot = placed[...] == there * cap + iota((cap, stations), 0)
        matrix = jnp.where(slot_hot, 1.0, 0.0).astype(jnp.bfloat16)
        packed = jnp.dot(matrix, ext[...], preferred_element_type=jnp.float32)
        box[code, :cap, :] = packed[:, :LANES].astype(jnp.bfloat16)
        turned = packed[:, LANES:].T
        for n in range(pages):
            box[code, cap + n * META : cap + (n + 1) * META, :page] = turned[
                :META, n * page : (n + 1) * page
            ].astype(jnp.bfloat16)

    def pack_and_send(turn, carry):
        code = order(turn, tiles)
        pack(code, partner(code), sent)
        obs_copy(code).start()
        return carry

    lax.fori_loop(0, tiles - 1, pack_and_send, 0)
    pack(0, me, got)

    def weigh(code):
        sheets = [
            got[code, cap + n * META : cap + (n + 1) * META, :][:, :page].astype(jnp.float32)
            for n in range(pages)
        ]
        meta = sheets[0] if pages == 1 else jnp.concatenate(sheets, axis=1)
        key = meta[steps + 1 : steps + 2] * rows + meta[steps : steps + 1]
        return key.astype(jnp.int32) == iota((rows * chunks, cap), 0), meta

    def spread(code, first):
        near, far = weigh(code), weigh(code + 1)
        for moment in range(steps):
            summed = None
            for n, (hot, meta) in enumerate((near, far)):
                weighted = jnp.where(hot, meta[moment : moment + 1], 0.0).astype(jnp.bfloat16)
                term = jnp.dot(
                    weighted, got[code + n, :cap, :], preferred_element_type=jnp.float32
                )
                summed = term if summed is None else summed + term
            for c in range(chunks):
                cells = (moment, own, slice(c * LANES, (c + 1) * LANES))
                piece = summed[c * rows : (c + 1) * rows]
                field[cells] = piece if first else field[cells] + piece

    for load in loads[4:]:
        load.wait()
    for side in range(2):
        rim = slice(RIM + rows, wide) if side == 0 else slice(0, RIM)

        @pl.when(exists[1 - side])
        def _():
            cel_copy(side).wait_recv()

        @pl.when(jnp.logical_not(exists[1 - side]))
        def _():
            kappa_ref[rim] = jnp.zeros((RIM, lat), jnp.float32)
            field[:, rim] = jnp.zeros((steps, RIM, lat), jnp.float32)

    kappa = kappa_ref[...]
    column = iota((wide, lat), 1)
    north = 0.5 * (kappa + pltpu.roll(kappa, 1, 0))
    south = 0.5 * (kappa + pltpu.roll(kappa, wide - 1, 0))
    west_edge, east_edge = column == 0, column == lat - 1
    west = 0.5 * (kappa + jnp.where(west_edge, 0.0, pltpu.roll(kappa, 1, 1)))
    east = 0.5 * (kappa + jnp.where(east_edge, 0.0, pltpu.roll(kappa, lat - 1, 1)))
    coef[0] = 2.0 - (north + south + west + east)
    coef[1] = north
    coef[2] = south
    coef[3] = jnp.where(west_edge, 0.0, west)
    coef[4] = jnp.where(east_edge, 0.0, east)

    moment = lax.div(iota((steps * LANES, LANES), 0), LANES).astype(jnp.float32)
    window = iota((steps * LANES, LANES), 1)
    tent_at = lax.rem(window, NWIN).astype(jnp.float32) * (steps - 1) / (NWIN - 1)
    tent = jnp.maximum(0.0, 1.0 - jnp.abs(moment - tent_at))
    for rake in range(2):
        basis[rake] = jnp.where(lax.div(window, NWIN) == rake, tent, 0.0)

    obs_copy(1).wait_recv()
    spread(0, True)

    def receive(pair, carry):
        obs_copy(2 * pair).wait_recv()
        obs_copy(2 * pair + 1).wait_recv()
        spread(2 * pair, False)
        return carry

    lax.fori_loop(1, tiles // 2, receive, 0)

    last = steps - 1
    level = iota((RIM, lat), 0)
    for n in range(steps // 2):
        t = last - n
        head, tail = field[t, own][:RIM], field[last - t, own][:RIM]
        rim_out[0, n] = jnp.where(level < t, head, pltpu.roll(tail, t, 0))
        head, tail = field[t, own][rows - RIM :], field[last - t, own][rows - RIM :]
        rim_out[1, n] = jnp.where(level >= RIM - t, head, pltpu.roll(tail, RIM - t, 0))
        for side in range(2):

            @pl.when(exists[side])
            def _():
                rim_copy(side, n).start()

    def land(n):
        t = last - n
        for side in range(2):

            @pl.when(exists[1 - side])
            def _():
                rim_copy(side, n).wait_recv()
                tile = rim_in[side, n]
                if side == 0:
                    rim = slice(RIM + rows, wide)
                    field[t, rim] = jnp.where(level < t, tile, 0.0)
                    field[last - t, rim] = jnp.where(
                        level < last - t, pltpu.roll(tile, RIM - t, 0), 0.0
                    )
                else:
                    rim = slice(0, RIM)
                    field[t, rim] = jnp.where(level >= RIM - t, tile, 0.0)
                    field[last - t, rim] = jnp.where(level > t, pltpu.roll(tile, t, 0), 0.0)

    line = iota((wide, lat), 0) + (me * rows - RIM)
    inside = jnp.logical_and(line >= 0, line < tiles * rows)

    def keep(t, surface):
        for c in range(chunks):
            past[t, c] = surface[own, c * LANES : (c + 1) * LANES]

    def advance(step, carry):
        t = last - step
        current = field[t + 1]
        moved = (
            coef[0] * current
            + coef[1] * pltpu.roll(current, 1, 0)
            + coef[2] * pltpu.roll(current, wide - 1, 0)
            + coef[3] * pltpu.roll(current, 1, 1)
            + coef[4] * pltpu.roll(current, lat - 1, 1)
            + field[t]
        )
        if not isinstance(step, int) or step > 1:
            moved = moved - field[t + 2]
        fresh = jnp.where(inside, moved, 0.0)
        field[t] = fresh
        keep(t, fresh)
        return carry

    land(0)
    keep(last, field[last])
    for n in range(1, steps // 2):
        land(n)
        advance(n, 0)
    lax.fori_loop(steps // 2, steps, advance, 0)
    out_ref[...] = field[0, own]

    def pick(segment, carry):
        block = segb_ref[segment]
        line, chunk = lax.div(block, chunks), lax.rem(block, chunks)
        for t in range(steps):
            picks[t, pl.ds(segment, 1)] = past[t, chunk, pl.ds(line, 1)]
        return carry

    lax.fori_loop(0, segments, pick, 0)

    lines = tiles * 8
    number = iota((lines, segments), 0)
    fault = jnp.where(
        lax.rem(number, 8) < SUB_DEV, lax.div(number, 8) * SUB_DEV + lax.rem(number, 8), -1
    )
    owner_hot = jnp.where(segf_ref[...] == fault, 1.0, 0.0)
    green = green_ref[...].astype(jnp.float32)
    total = None
    for rake in range(2):
        weights = green[:, rake * LANES : (rake + 1) * LANES]
        products = jnp.concatenate([picks[t] * weights for t in range(steps)], axis=1)
        by_fault = jnp.dot(owner_hot, products, precision=HIGH, preferred_element_type=jnp.float32)
        term = jnp.dot(by_fault, basis[rake], precision=HIGH, preferred_element_type=jnp.float32)
        total = term if total is None else total + term
    part_out[...] = total.reshape(tiles, 8, LANES)

    def part_copy(code):
        there = partner(code)
        return pltpu.make_async_remote_copy(
            src_ref=part_out.at[there],
            dst_ref=part_in.at[code],
            send_sem=part_send.at[code],
            recv_sem=part_recv.at[code],
            device_id={"lon": there},
            device_id_type=pl.DeviceIdType.MESH,
        )

    def part_start(turn, carry):
        part_copy(order(turn, tiles)).start()
        return carry

    lax.fori_loop(0, tiles - 1, part_start, 0)
    part_in[0] = part_out[me]

    def sent_wait(code, carry):
        obs_copy(code).wait_send()
        return carry

    lax.fori_loop(1, tiles, sent_wait, 0)
    for side in range(2):

        @pl.when(exists[side])
        def _():
            cel_copy(side).wait_send()
            for n in range(steps // 2):
                rim_copy(side, n).wait_send()

    def part_wait(code, carry):
        part_copy(code).wait()
        return carry

    lax.fori_loop(1, tiles, part_wait, 0)
    grad_ref[...] = jnp.sum(part_in[...], axis=0)[:SUB_DEV, : 2 * NWIN]


def local(
    celerity,
    station_tile,
    station_block,
    footprint,
    misfit,
    segment_block,
    segment_fault,
    green_uplift,
):
    tiles = lax.axis_size("lon")
    rows, lat = celerity.shape
    stations = footprint.shape[0]
    steps = misfit.shape[0]
    segments = green_uplift.shape[0]
    cap = 2 * stations // tiles
    depth = cap + META * -(-cap // LANES)
    dma = pltpu.SemaphoreType.DMA
    vmem = pl.BlockSpec(memory_space=pltpu.VMEM)
    return pl.pallas_call(
        functools.partial(kernel, tiles, cap),
        out_shape=(
            jax.ShapeDtypeStruct((rows, lat), jnp.float32),
            jax.ShapeDtypeStruct((SUB_DEV, 2 * NWIN), jnp.float32),
        ),
        in_specs=[pl.BlockSpec(memory_space=pltpu.HBM)] * 8,
        out_specs=(vmem, vmem),
        scratch_shapes=[
            pltpu.VMEM((1, stations), jnp.int32),
            pltpu.VMEM((1, stations), jnp.int32),
            pltpu.VMEM((steps, stations), jnp.bfloat16),
            pltpu.SMEM((segments,), jnp.int32),
            pltpu.VMEM((1, segments), jnp.int32),
            pltpu.VMEM((segments, 2 * LANES), jnp.bfloat16),
            pltpu.VMEM((rows + 2 * RIM, lat), jnp.float32),
            pltpu.VMEM((5, rows + 2 * RIM, lat), jnp.float32),
            pltpu.VMEM((2, steps * LANES, LANES), jnp.float32),
            dma((8,)),
            pltpu.VMEM((stations, 2 * LANES), jnp.bfloat16),
            pltpu.VMEM((1, stations), jnp.int32),
            pltpu.VMEM((tiles, depth, LANES), jnp.bfloat16),
            pltpu.VMEM((tiles, depth, LANES), jnp.bfloat16),
            pltpu.VMEM((steps, rows + 2 * RIM, lat), jnp.float32),
            pltpu.VMEM((2, steps // 2, RIM, lat), jnp.float32),
            pltpu.VMEM((2, steps // 2, RIM, lat), jnp.float32),
            pltpu.VMEM((steps, lat // LANES, rows, LANES), jnp.float32),
            pltpu.VMEM((steps, segments, LANES), jnp.float32),
            pltpu.VMEM((tiles, 8, LANES), jnp.float32),
            pltpu.VMEM((tiles, 8, LANES), jnp.float32),
            dma((tiles,)),
            dma((tiles,)),
            dma((steps // 2, 2)),
            dma((steps // 2, 2)),
            dma((1, 2)),
            dma((1, 2)),
            dma((tiles,)),
            dma((tiles,)),
        ],
        compiler_params=pltpu.CompilerParams(
            collective_id=0, has_side_effects=True, vmem_limit_bytes=44 * 1024 * 1024
        ),
    )(
        celerity,
        station_tile.reshape(1, stations),
        station_block.reshape(1, stations),
        footprint,
        misfit,
        segment_block,
        segment_fault.reshape(1, segments),
        green_uplift,
    )


def solution(mesh):
    placed = (
        P("lon", None),
        P(("groups", "lon"), None),
        P(("groups", "lon")),
        P(("groups", "lon"), None),
        P(None, ("groups", "lon")),
        P("lon"),
        P("lon"),
        P("lon", None),
    )
    return jax.shard_map(
        local,
        mesh=mesh,
        in_specs=placed,
        out_specs=(P(("groups", "lon"), None), P(("groups", "lon"), None)),
        check_vma=False,
    )
```

time: 63.7 us -> 59.1 us (0.928)
  Pallas kernels: 55.8 us -> 51.2 us
    pallas_call x1, Pallas kernels: 55.8 us -> 51.2 us  [local(): pl.pallas_call(functools.partial(kernel, tiles, cap), out_shape=(jax.Shap...]
where the time goes in v1:
time: 59.1 us; the launch traced here: 58.7 us
  Pallas kernels  51.2 us (87%)
  local copies, waits for them, and re-layouts  6.84 us (12%)
  between operations  0.66 us (1%)
    pallas_call x1, Pallas kernels, local(): pl.pallas_call(functools.partial(kernel, tiles, cap), out_shape=(jax.Shap...  51.2 us
    unnamed x18, local copies, waits for them, and re-layouts  6.84 us

profile of v1, /device:TPU:0, one launch (start us, length us, event | category | flops | bytes accessed | tf_op | source)
XLA Modules:
  0.0 58.7 jit_solution(9067692495683228388)
XLA Ops:
  0.6 0.0 copy-start.6
  0.6 0.0 copy-start.7
  0.7 0.6 %copy-done.6 = s32[64]{0:T(128)S(1)} copy-done((s32[64]{0:T(128)S(1)}, s32[64]{0:T(128)}, u32[]{:S(2)}) %copy-start.6) | copy-done | bytes 280
  1.3 0.0 copy-done.7
  1.3 0.0 copy-start
  1.3 1.0 %copy-done = bf16[2048,128]{1,0:T(8,128)(2,1)S(1)} copy-done((bf16[2048,128]{1,0:T(8,128)(2,1)S(1)}, bf16[2048,128]{1,0:T(8,128)(2,1)}, u32[]{:S(2)}) %copy-start) | copy-done | bytes 524312
  2.3 0.0 copy-start.1
  2.3 0.9 %copy-done.1 = f32[32,2048]{1,0:T(8,128)S(1)} copy-done((f32[32,2048]{1,0:T(8,128)S(1)}, f32[32,2048]{1,0:T(8,128)}, u32[]{:S(2)}) %copy-start.1) | copy-done | bytes 262168
  3.3 0.0 copy-start.2
  3.3 0.8 %copy-done.2 = bf16[8,2048]{1,0:T(8,128)(2,1)S(1)} copy-done((bf16[8,2048]{1,0:T(8,128)(2,1)S(1)}, bf16[8,2048]{1,0:T(8,128)(2,1)}, u32[]{:S(2)}) %copy-start.2) | copy-done | bytes 32792
  4.1 0.0 copy-start.3
  4.1 0.8 %copy-done.3 = bf16[64,256]{1,0:T(8,128)(2,1)S(1)} copy-done((bf16[64,256]{1,0:T(8,128)(2,1)S(1)}, bf16[64,256]{1,0:T(8,128)(2,1)}, u32[]{:S(2)}) %copy-start.3) | copy-done | bytes 32792
  4.8 0.0 copy-start.4
  4.8 0.7 %copy-done.4 = s32[2048,1]{0,1:T(1,128)S(1)} copy-done((s32[2048,1]{0,1:T(1,128)S(1)}, s32[2048,1]{0,1:T(1,128)}, u32[]{:S(2)}) %copy-start.4) | copy-done | bytes 8216
  5.5 0.0 copy-start.5
  5.5 0.7 %copy-done.5 = s32[2048]{0:T(1024)S(1)} copy-done((s32[2048]{0:T(1024)S(1)}, s32[2048]{0:T(1024)}, u32[]{:S(2)}) %copy-start.5) | copy-done | bytes 8216
  6.2 51.2 %shard_map.95 = (f32[32,2048]{1,0:T(8,128)S(1)}, f32[4,64]{1,0:T(4,128)S(1)}) custom-call(f32[32,2048]{1,0:T(8,128)S(1)} %copy-done.1, s32[1,2048]{1,0:T(1,128)S(1)} %bitcast.3, s32[1,2048]{1,0:T(1,128)S(1)} %bitcast.4, bf16[2048,128]{1,0:T(8,128)(2,1)S(1)} %copy-done, bf16[8,2048]{1,0:T(8,128)(2,1)S(1)} %copy-done.2, s32[64]{0:T(128)S(1)} %copy-done.6, ...), custom_call_target="tpu_custom_call" | custom-call | tf_op jit(solution)/shard_map/pallas_call | solution.py:428
  57.4 0.7 %copy.12 = f32[32,2048]{1,0:T(8,128)} copy(f32[32,2048]{1,0:T(8,128)S(1)} %get-tuple-element.4) | data formatting | bytes 524288
  58.1 0.6 copy.13
Async XLA Ops:
  0.6 0.7 %copy-start.6 = (s32[64]{0:T(128)S(1)}, s32[64]{0:T(128)}, u32[]{:S(2)}) copy-start(s32[64]{0:T(128)} %segb_hbm.1) | copy-start | bytes 772
  0.6 0.7 %copy-start.7 = (s32[64]{0:T(128)S(1)}, s32[64]{0:T(128)}, u32[]{:S(2)}) copy-start(s32[64]{0:T(128)} %param.14) | copy-start | bytes 772
  1.3 1.0 %copy-start = (bf16[2048,128]{1,0:T(8,128)(2,1)S(1)}, bf16[2048,128]{1,0:T(8,128)(2,1)}, u32[]{:S(2)}) copy-start(bf16[2048,128]{1,0:T(8,128)(2,1)} %foot_hbm.1) | copy-start | bytes 1572868
  2.3 0.9 %copy-start.1 = (f32[32,2048]{1,0:T(8,128)S(1)}, f32[32,2048]{1,0:T(8,128)}, u32[]{:S(2)}) copy-start(f32[32,2048]{1,0:T(8,128)} %cel_hbm.1) | copy-start | bytes 786436
  3.3 0.8 %copy-start.2 = (bf16[8,2048]{1,0:T(8,128)(2,1)S(1)}, bf16[8,2048]{1,0:T(8,128)(2,1)}, u32[]{:S(2)}) copy-start(bf16[8,2048]{1,0:T(8,128)(2,1)} %mis_hbm.1) | copy-start | bytes 98308
  4.1 0.8 %copy-start.3 = (bf16[64,256]{1,0:T(8,128)(2,1)S(1)}, bf16[64,256]{1,0:T(8,128)(2,1)}, u32[]{:S(2)}) copy-start(bf16[64,256]{1,0:T(8,128)(2,1)} %green_hbm.1) | copy-start | bytes 98308
  4.8 0.7 %copy-start.4 = (s32[2048,1]{0,1:T(1,128)S(1)}, s32[2048,1]{0,1:T(1,128)}, u32[]{:S(2)}) copy-start(s32[2048,1]{0,1:T(1,128)} %param.9) | copy-start | bytes 24580
  5.5 0.7 %copy-start.5 = (s32[2048]{0:T(1024)S(1)}, s32[2048]{0:T(1024)}, u32[]{:S(2)}) copy-start(s32[2048]{0:T(1024)} %param.10) | copy-start | bytes 24580

commit v2 on v1

--- a/solution.py
+++ b/solution.py
@@ -97,23 +97,34 @@
     for load in loads:
         load.start()
 
+    units = [1 << n for n in range(tiles.bit_length() - 1)]
+    bits = [lax.rem(lax.div(me, unit), 2) for unit in units]
+
     def partner(code):
-        there, unit = 0, 1
-        while unit < tiles:
-            there += lax.rem(lax.div(me, unit) + lax.div(code, unit), 2) * unit
-            unit *= 2
+        there = me
+        for unit, bit in zip(units, bits):
+            if isinstance(code, int):
+                there = there + (unit - 2 * unit * bit if code & unit else 0)
+            else:
+                there = there + lax.rem(lax.div(code, unit), 2) * (unit - 2 * unit * bit)
         return there
 
-    def greet(shift, carry):
+    def others(work):
+        if tiles <= 16:
+            for turn in range(tiles - 1):
+                work(tiles // 2 + turn // 2 if turn % 2 == 0 else turn // 2 + 1)
+        else:
+            lax.fori_loop(1, tiles, lambda code, carry: (work(code), carry)[1], 0)
+
+    def greet(code):
         pl.semaphore_signal(
             barrier,
             inc=1,
-            device_id={"lon": partner(shift)},
+            device_id={"lon": partner(code)},
             device_id_type=pl.DeviceIdType.MESH,
         )
-        return carry
-
-    lax.fori_loop(1, tiles, greet, 0)
+
+    others(greet)
     for load in loads[:3]:
         load.wait()
 
@@ -147,8 +158,6 @@
     ext[:, LANES:] = meta.T.astype(jnp.bfloat16)
     loads[3].wait()
 
-    pl.semaphore_wait(barrier, tiles - 1)
-
     def side_copy(side, source, landing, send, recv):
         return pltpu.make_async_remote_copy(
             src_ref=source,
@@ -170,12 +179,6 @@
         return side_copy(
             side, rim_out.at[side, n], rim_in.at[side, n], rim_send.at[n], rim_recv.at[n]
         )
-
-    for side in range(2):
-
-        @pl.when(exists[side])
-        def _():
-            cel_copy(side).start()
 
     def obs_copy(code):
         return pltpu.make_async_remote_copy(
@@ -204,7 +207,16 @@
         obs_copy(code).start()
         return carry
 
-    lax.fori_loop(0, tiles - 1, pack_and_send, 0)
+    pack(tiles // 2, partner(tiles // 2), sent)
+    pl.semaphore_wait(barrier, tiles - 1)
+    for side in range(2):
+
+        @pl.when(exists[side])
+        def _():
+            cel_copy(side).start()
+
+    obs_copy(tiles // 2).start()
+    lax.fori_loop(1, tiles - 1, pack_and_send, 0)
     pack(0, me, got)
 
     def weigh(code):
@@ -378,18 +390,10 @@
             device_id_type=pl.DeviceIdType.MESH,
         )
 
-    def part_start(turn, carry):
-        part_copy(order(turn, tiles)).start()
-        return carry
-
-    lax.fori_loop(0, tiles - 1, part_start, 0)
+    others(lambda code: part_copy(code).start())
     part_in[0] = part_out[me]
 
-    def sent_wait(code, carry):
-        obs_copy(code).wait_send()
-        return carry
-
-    lax.fori_loop(1, tiles, sent_wait, 0)
+    others(lambda code: obs_copy(code).wait_send())
     for side in range(2):
 
         @pl.when(exists[side])
@@ -398,11 +402,7 @@
             for n in range(steps // 2):
                 rim_copy(side, n).wait_send()
 
-    def part_wait(code, carry):
-        part_copy(code).wait()
-        return carry
-
-    lax.fori_loop(1, tiles, part_wait, 0)
+    others(lambda code: part_copy(code).wait())
     grad_ref[...] = jnp.sum(part_in[...], axis=0)[:SUB_DEV, : 2 * NWIN]
 
 
@@ -465,7 +465,7 @@
             dma((tiles,)),
         ],
         compiler_params=pltpu.CompilerParams(
-            collective_id=0, has_side_effects=True, vmem_limit_bytes=44 * 1024 * 1024
+            collective_id=0, has_side_effects=True, vmem_limit_bytes=64 * 1024 * 1024
         ),
     )(
         celerity,

time: 59.1 us -> 54.2 us (0.917)
  local copies, waits for them, and re-layouts: 6.84 us -> 2.25 us
    unnamed x18 -> x4, local copies, waits for them, and re-layouts: 6.84 us -> 2.25 us
where the time goes in v2:
time: 54.2 us; the launch traced here: 54 us
  Pallas kernels  51.1 us (94%)
  local copies, waits for them, and re-layouts  2.25 us (4%)
  between operations  0.65 us (1%)
    pallas_call x1, Pallas kernels, local(): pl.pallas_call(functools.partial(kernel, tiles, cap), out_shape=(jax.Shap...  51.1 us
    unnamed x4, local copies, waits for them, and re-layouts  2.25 us

profile of v2, /device:TPU:0, one launch (start us, length us, event | category | flops | bytes accessed | tf_op | source)
XLA Modules:
  0.0 54.0 jit_solution(15517767698593069512)
XLA Ops:
  0.6 51.1 %shard_map.95 = (f32[32,2048]{1,0:T(8,128)}, f32[4,64]{1,0:T(4,128)}) custom-call(f32[32,2048]{1,0:T(8,128)} %cel_hbm.1, s32[1,2048]{1,0:T(1,128)} %bitcast.3, s32[1,2048]{1,0:T(1,128)} %bitcast.4, bf16[2048,128]{1,0:T(8,128)(2,1)} %foot_hbm.1, bf16[8,2048]{1,0:T(8,128)(2,1)} %mis_hbm.1, s32[64]{0:T(128)} %segb_hbm.1, s32[1,64]{1,0:T(1,128)} %bitcast.5, ...), custom_call_target="tpu_custom_call" | custom-call | tf_op jit(solution)/shard_map/pallas_call | solution.py:428
  51.7 0.0 copy-start
  51.7 1.7 %copy.12 = f32[32,2048]{1,0:T(8,128)} copy(f32[32,2048]{1,0:T(8,128)} %get-tuple-element.4) | data formatting | bytes 524288
  53.4 0.0 copy-done
  53.4 0.6 %copy.13 = f32[4,64]{1,0:T(4,128)} copy(f32[4,64]{1,0:T(4,128)S(1)} %copy-done) | data formatting | bytes 2048
Async XLA Ops:
  51.7 1.7 %copy-start = (f32[4,64]{1,0:T(4,128)S(1)}, f32[4,64]{1,0:T(4,128)}, u32[]{:S(2)}) copy-start(f32[4,64]{1,0:T(4,128)} %get-tuple-element.5) | copy-start | bytes 3076

commit v3 on v2

--- a/solution.py
+++ b/solution.py
@@ -352,7 +352,8 @@
         land(n)
         advance(n, 0)
     lax.fori_loop(steps // 2, steps, advance, 0)
-    out_ref[...] = field[0, own]
+    store = pltpu.make_async_copy(field.at[0, pl.ds(RIM, rows)], out_ref, load_sem.at[len(loads)])
+    store.start()
 
     def pick(segment, carry):
         block = segb_ref[segment]
@@ -403,6 +404,7 @@
                 rim_copy(side, n).wait_send()
 
     others(lambda code: part_copy(code).wait())
+    store.wait()
     grad_ref[...] = jnp.sum(part_in[...], axis=0)[:SUB_DEV, : 2 * NWIN]
 
 
@@ -432,7 +434,7 @@
             jax.ShapeDtypeStruct((SUB_DEV, 2 * NWIN), jnp.float32),
         ),
         in_specs=[pl.BlockSpec(memory_space=pltpu.HBM)] * 8,
-        out_specs=(vmem, vmem),
+        out_specs=(pl.BlockSpec(memory_space=pltpu.HBM), vmem),
         scratch_shapes=[
             pltpu.VMEM((1, stations), jnp.int32),
             pltpu.VMEM((1, stations), jnp.int32),
@@ -443,7 +445,7 @@
             pltpu.VMEM((rows + 2 * RIM, lat), jnp.float32),
             pltpu.VMEM((5, rows + 2 * RIM, lat), jnp.float32),
             pltpu.VMEM((2, steps * LANES, LANES), jnp.float32),
-            dma((8,)),
+            dma((9,)),
             pltpu.VMEM((stations, 2 * LANES), jnp.bfloat16),
             pltpu.VMEM((1, stations), jnp.int32),
             pltpu.VMEM((tiles, depth, LANES), jnp.bfloat16),

time: 54.2 us -> 54.1 us (level)
  no operation moved by 1% of the time
where the time goes in v3:
time: 54.1 us; the launch traced here: 53.9 us
  Pallas kernels  51 us (94%)
  local copies, waits for them, and re-layouts  2.25 us (4%)
  between operations  0.65 us (1%)
    pallas_call x1, Pallas kernels, local(): pl.pallas_call(functools.partial(kernel, tiles, cap), out_shape=(jax.Shap...  51 us
    unnamed x4, local copies, waits for them, and re-layouts  2.25 us

profile of v3, /device:TPU:0, one launch (start us, length us, event | category | flops | bytes accessed | tf_op | source)
XLA Modules:
  0.0 53.9 jit_solution(7704245265524501903)
XLA Ops:
  0.6 51.0 %shard_map.95 = (f32[32,2048]{1,0:T(8,128)}, f32[4,64]{1,0:T(4,128)}) custom-call(f32[32,2048]{1,0:T(8,128)} %cel_hbm.1, s32[1,2048]{1,0:T(1,128)} %bitcast.3, s32[1,2048]{1,0:T(1,128)} %bitcast.4, bf16[2048,128]{1,0:T(8,128)(2,1)} %foot_hbm.1, bf16[8,2048]{1,0:T(8,128)(2,1)} %mis_hbm.1, s32[64]{0:T(128)} %segb_hbm.1, s32[1,64]{1,0:T(1,128)} %bitcast.5, ...), custom_call_target="tpu_custom_call" | custom-call | tf_op jit(solution)/shard_map/pallas_call | solution.py:430
  51.6 0.0 copy-start
  51.6 1.7 %copy.12 = f32[32,2048]{1,0:T(8,128)} copy(f32[32,2048]{1,0:T(8,128)} %get-tuple-element.4) | data formatting | bytes 524288
  53.3 0.0 copy-done
  53.3 0.6 %copy.13 = f32[4,64]{1,0:T(4,128)} copy(f32[4,64]{1,0:T(4,128)S(1)} %copy-done) | data formatting | bytes 2048
Async XLA Ops:
  51.6 1.7 %copy-start = (f32[4,64]{1,0:T(4,128)S(1)}, f32[4,64]{1,0:T(4,128)}, u32[]{:S(2)}) copy-start(f32[4,64]{1,0:T(4,128)} %get-tuple-element.5) | copy-start | bytes 3076
